TPU v7x, 512 devices: a whole 4x8x8 slice. The times are simulated.
512 devices in a mesh: tensor: 32 (over z, y_hi, core), replay: 16 (over x, y_lo).
Axes of the slice: x: 4, y: 8 (y_hi: 2, y_lo: 4; y = y_hi * 4 + y_lo), z: 8, core: 2. Of those that a mesh axis runs over, the one named last changes fastest.
Arguments:
- x_store: bfloat16 [2048, 4096], P('replay', 'tensor'), may hold values from -6 to 6
- attn_store: bfloat16 [2048, 4096], P('replay', 'tensor'), may hold values from -6 to 6
- replay_idx: int32 [16, 128], P('replay'), may hold values from 0 to 127
- w_qkv: bfloat16 [6144, 4096], P('tensor', 'replay'), may hold values from -0.09375 to 0.09375
- w_out: bfloat16 [4096, 4096], P('tensor', 'replay'), may hold values from -0.09375 to 0.09375
- d_qkv: bfloat16 [2048, 6144], P('replay', 'tensor'), may hold values from -6 to 6
- d_out: bfloat16 [2048, 4096], P('replay', 'tensor'), may hold values from -6 to 6
Outputs:
- qkv: float32 [2048, 6144], P('replay', 'tensor')
- out: float32 [2048, 4096], P('replay', 'tensor')
- grad_inputs: float32 [2048, 4096], P('replay', 'tensor')
- grad_attn: float32 [2048, 4096], P('replay', 'tensor')
- grad_wqkv: bfloat16 [6144, 4096], P('tensor')
- grad_wout: bfloat16 [4096, 4096], P('tensor')
Inputs may be any that keep to these rules, and one draw needn't show every extreme that they name: `replay_idx`: rows are sampled with replacement within each group's store of 128 rows.
All inputs are finite; a program needn't handle non-finite values.
Results may differ from a plain program's by a relative error of at most 0.023.
Values may be sent and summed in bfloat16 or wider, within the bound.
A program may use at most 64 MiB of HBM per device.

v0:
```python
import jax
import jax.numpy as jnp
from jax import lax
from jax.sharding import PartitionSpec as P


def shards(x_store, attn_store, replay_idx, w_qkv, w_out, d_qkv, d_out):
    picked = replay_idx[0]
    inputs = jnp.take(x_store, picked, axis=0)
    heads = jnp.take(attn_store, picked, axis=0)
    count_rows = inputs.shape[0]
    factor = 1.0 / count_rows
    qkv_full, out_full = (
        lax.all_gather(w_qkv, "replay", axis=1, tiled=True),
        lax.all_gather(w_out, "replay", axis=1, tiled=True),
    )
    piece = lax.all_gather(inputs, "tensor", axis=1, tiled=True)
    w_cols = qkv_full
    total = lax.dot_general(
        piece, w_cols, (((1,), (1,)), ((), ())), preferred_element_type=jnp.float32
    )
    block = lax.dot_general(
        d_qkv, piece, (((0,), (0,)), ((), ())), preferred_element_type=jnp.float32
    )
    grad = block
    qkv_total = total
    grad_qkv_part = grad
    piece = lax.all_gather(d_out, "tensor", axis=1, tiled=True)
    w_cols = out_full
    total = lax.dot_general(
        piece, w_cols, (((1,), (1,)), ((), ())), preferred_element_type=jnp.float32
    )
    block = lax.dot_general(
        heads, piece, (((0,), (0,)), ((), ())), preferred_element_type=jnp.float32
    )
    grad = block
    out_part = jnp.dot(heads, out_full, preferred_element_type=jnp.float32)
    out = lax.psum_scatter(
        out_part.astype(jnp.bfloat16), "tensor", scatter_dimension=1, tiled=True
    ).astype(jnp.float32)
    input_part = jnp.dot(d_qkv, qkv_full, preferred_element_type=jnp.float32)
    grad_inputs = lax.psum_scatter(
        input_part.astype(jnp.bfloat16), "tensor", scatter_dimension=1, tiled=True
    ).astype(jnp.float32)
    summed_qkv, summed_out = (
        lax.psum((grad_qkv_part * factor).astype(jnp.bfloat16), "replay").astype(jnp.float32),
        lax.psum((grad * factor).astype(jnp.bfloat16), "replay").astype(jnp.float32),
    )
    return (
        qkv_total,
        out,
        grad_inputs,
        total,
        summed_qkv.astype(jnp.bfloat16),
        summed_out.astype(jnp.bfloat16),
    )


def solution(mesh):
    in_specs = (
        P("replay", "tensor"),
        P("replay", "tensor"),
        P("replay", None),
        P("tensor", "replay"),
        P("tensor", "replay"),
        P("replay", "tensor"),
        P("replay", "tensor"),
    )
    out_specs = (
        P("replay", "tensor"),
        P("replay", "tensor"),
        P("replay", "tensor"),
        P("replay", "tensor"),
        P("tensor", None),
        P("tensor", None),
    )
    return jax.shard_map(shards, mesh=mesh, in_specs=in_specs, out_specs=out_specs, check_vma=False)
```

profile of v0, /device:TPU:1, one launch (start us, length us, event | category | flops | bytes accessed | tf_op | source)
XLA Modules:
  0.0 778.4 jit_solution(2391926083000397346)
XLA Ops:
  7.2 0.0 copy-start
  7.2 0.0 all-gather.9.cloned.1.call-start
  7.2 0.7 all-gather.9.cloned.1.call-update
  7.9 0.0 all-gather.7.cloned.1.call-start
  8.0 0.7 all-gather.7.cloned.1.call-update
  8.7 0.0 all-gather.11.cloned.1.call-start
  8.7 0.7 all-gather.11.cloned.1.call-update
  9.4 0.0 all-gather.5.cloned.1.call-start
  9.4 0.7 compare_select_fusion
  10.1 1.4 gather_fusion
  11.5 0.7 compare_and_fusion
  12.2 0.7 broadcast_select_fusion.1
  12.9 0.0 all-gather.5.cloned.1.call-update
  12.9 0.0 reduce-scatter.7.cloned.1.call-start
  13.0 1.4 gather_fusion.1
  14.4 66.2 %all-gather.9.cloned.1.call-done = bf16[128,4096]{1,0:T(8,128)(2,1)} async-done(((bf16[128,256]{1,0:T(8,128)(2,1)}), bf16[128,4096]{1,0:T(8,128)(2,1)}) %all-gather.9.cloned.1.call-update) | async-done | bytes 1048592 | tf_op jit(solution)/shard_map/all_gather | solution.py:15
  80.6 1.7 convolution_convert_fusion.1
  82.3 1.3 copy.13
  83.6 0.0 reduce-scatter.7.cloned.1.call-update
  83.6 0.0 reduce-scatter.9.cloned.1.call-start
  83.7 77.6 %all-gather.7.cloned.1.call-done = bf16[192,4096]{1,0:T(8,128)(2,1)} async-done(((bf16[192,256]{1,0:T(8,128)(2,1)}), bf16[192,4096]{1,0:T(8,128)(2,1)}) %all-gather.7.cloned.1.call-update) | async-done | bytes 1572880 | tf_op jit(solution)/shard_map/all_gather | solution.py:14
  161.3 0.0 copy-done
  161.3 1.9 convolution_convert_fusion
  163.2 1.3 copy.15
  164.5 0.0 reduce-scatter.9.cloned.1.call-update
  164.5 0.0 all-reduce.3.cloned.1.call-start
  164.6 89.2 %all-gather.11.cloned.1.call-done = bf16[128,4096]{1,0:T(8,128)(2,1)} async-done(((bf16[128,128]{1,0:T(8,128)(2,1)}), bf16[128,4096]{1,0:T(8,128)(2,1)}) %all-gather.11.cloned.1.call-update) | async-done | bytes 1048592 | tf_op jit(solution)/shard_map/all_gather | solution.py:28
  253.8 2.7 fusion.1
  256.5 77.9 %all-gather.5.cloned.1.call-done = bf16[128,4096]{1,0:T(8,128)(2,1)} async-done(((bf16[128,128]{1,0:T(8,128)(2,1)}), bf16[128,4096]{1,0:T(8,128)(2,1)}) %all-gather.5.cloned.1.call-update) | async-done | bytes 1048592 | tf_op jit(solution)/shard_map/all_gather | solution.py:17
  334.3 2.9 fusion.2
  337.3 0.0 copy-start.2
  337.3 0.0 copy-start.3
  337.3 0.0 copy-start.4
  337.3 0.0 all-reduce.3.cloned.1.call-update
  337.3 1.2 copy-done.2
  338.5 0.3 copy-done.3
  338.8 0.0 copy-start.1
  338.8 1.1 fusion.6
  339.9 0.0 copy-done.4
  339.9 0.4 copy-done.1
  340.3 1.2 fusion.5
  341.5 117.5 %reduce-scatter.7.cloned.1.call-done = bf16[128,128]{1,0:T(8,128)(2,1)} async-done(((bf16[4096,128]{1,0:T(8,128)(2,1)}), bf16[128,128]{1,0:T(8,128)(2,1)}) %reduce-scatter.7.cloned.1.call-update) | async-done | bytes 32784
  459.1 0.9 copy.14
  459.9 0.6 convert_element_type.26
  460.6 127.2 %reduce-scatter.9.cloned.1.call-done = bf16[128,128]{1,0:T(8,128)(2,1)} async-done(((bf16[4096,128]{1,0:T(8,128)(2,1)}), bf16[128,128]{1,0:T(8,128)(2,1)}) %reduce-scatter.9.cloned.1.call-update) | async-done | bytes 32784
  587.8 0.9 copy.16
  588.7 0.6 convert_element_type.28
  589.3 178.4 %all-reduce.3.cloned.1.call-done = (bf16[192,4096]{1,0:T(8,128)(2,1)}, bf16[128,4096]{1,0:T(8,128)(2,1)}) async-done(((bf16[192,4096]{1,0:T(8,128)(2,1)}, bf16[128,4096]{1,0:T(8,128)(2,1)}), (bf16[192,4096]{1,0:T(8,128)(2,1)}, bf16[128,4096]{1,0:T(8,128)(2,1)})) %all-reduce.3.cloned.1.call-update) | async-done | bytes 2621456 | tf_op jit(solution)/shard_map/psum | solution.py:46
  767.8 0.0 copy-start.5
  767.8 2.8 copy.19
  770.5 0.0 copy-done.5
  770.6 1.0 copy.20
  (1 shorter events, 0.0 us)
Async XLA Ops:
  7.2 154.1 %copy-start = (bf16[128,192]{0,1:T(8,128)(2,1)S(1)}, bf16[128,192]{0,1:T(8,128)(2,1)}, u32[]{:S(2)}) copy-start(bf16[128,192]{0,1:T(8,128)(2,1)} %param.14) | copy-start | bytes 147460
  7.2 73.4 %all-gather.9.cloned.1.call-start = ((), (), s32[]{:S(2)}) async-start(), calls=%async_computation.4 | async-start | bytes 1114112 | tf_op jit(solution)/shard_map/all_gather | solution.py:15
  7.9 153.4 %all-gather.7.cloned.1.call-start = ((), (), s32[]{:S(2)}) async-start(), calls=%async_computation.3 | async-start | bytes 1671168 | tf_op jit(solution)/shard_map/all_gather | solution.py:14
  8.7 245.1 %all-gather.11.cloned.1.call-start = ((), (), s32[]{:S(2)}) async-start(), calls=%async_computation.5 | async-start | bytes 1081344 | tf_op jit(solution)/shard_map/all_gather | solution.py:28
  9.4 324.9 %all-gather.5.cloned.1.call-start = ((), (), s32[]{:S(2)}) async-start(), calls=%async_computation.2 | async-start | bytes 1081344 | tf_op jit(solution)/shard_map/all_gather | solution.py:17
  12.9 446.1 %reduce-scatter.7.cloned.1.call-start = ((), (), s32[]{:S(2)}) async-start(), calls=%async_computation.6 | async-start | bytes 1081344
  83.6 504.2 %reduce-scatter.9.cloned.1.call-start = ((), (), s32[]{:S(2)}) async-start(), calls=%async_computation.7 | async-start | bytes 1081344
  164.5 603.3 %all-reduce.3.cloned.1.call-start = ((), (), s32[]{:S(2)}) async-start(), calls=%async_computation.8 | async-start | bytes 5242880 | tf_op jit(solution)/shard_map/psum | solution.py:46
  337.3 1.2 copy-start.2
  337.3 1.6 copy-start.3
  337.3 2.6 copy-start.4
  338.8 1.5 copy-start.1
  767.8 2.8 copy-start.5
Sparse Core Ops, SparseCore 0:
  10.0 70.5 all-gather.8
  82.6 78.6 all-gather.6
  164.4 89.2 all-gather.10
  257.3 76.9 all-gather.4
  339.4 119.5 reduce-scatter.6
  464.3 123.4 reduce-scatter.8
  591.4 176.3 all-reduce.2
where the time goes:
time: 787 us; the launch traced here: 778 us
  waiting for transfers between devices  736 us (94%)
  between operations  14.2 us (2%)
  local copies, waits for them, and re-layouts  12.9 us (2%)
  matrix products  11.5 us (1%)
    unnamed x9, waiting for transfers between devices  247 us
    psum x1, waiting for transfers between devices, shards(): lax.psum((grad_qkv_part * factor).astype(jnp.bfloat16), 'replay')  178 us
    all_gather x1, waiting for transfers between devices, shards(): piece = lax.all_gather(d_out, 'tensor', axis=1, tiled=True)  89.2 us
    all_gather x1, waiting for transfers between devices, shards(): piece = lax.all_gather(inputs, 'tensor', axis=1, tiled=True)  77.9 us
    all_gather x1, waiting for transfers between devices, shards(): lax.all_gather(w_qkv, 'replay', axis=1, tiled=True)  77.6 us
    all_gather x1, waiting for transfers between devices, shards(): lax.all_gather(w_out, 'replay', axis=1, tiled=True)  66.2 us
  transfers between devices with their start and end apart: 7, of which 7 were waited for; matrix products, arithmetic and copies ran while one was open for 3% of the time, Pallas kernels for 0%

commit v1 on v0

v1 whole, which is shorter than its diff:
```python
import jax
import jax.numpy as jnp
from jax import lax
from jax.experimental import pallas as pl
from jax.experimental.pallas import tpu as pltpu
from jax.sharding import PartitionSpec as P

BF, F32 = jnp.bfloat16, jnp.float32
MESH = pl.DeviceIdType.MESH
ROWS, QF, OF, QO = 128, 192, 128, 320
PARTS = ((0, QF), (QF, OF))


def dot(a, b, ca, cb):
    return lax.dot_general(a, b, (((ca,), (cb,)), ((), ())), preferred_element_type=F32)


def make_labels():
    table = {}

    def label(*key):
        return table.setdefault(key, len(table))

    return table, label


TABLE, LABEL = make_labels()


def kernel(x_ref, a_ref, idx_ref, wq_ref, wo_ref, dq_ref, do_ref,
           qkv_ref, out_ref, gin_ref, gat_ref, gwq_ref, gwo_ref,
           own, dh, wall, xb, gsend, gkeep, gacc, gr1, gr2, gout,
           ysend, yrecv, ykeep, esend, erecv, part, zsend, zrecv, scsend, screcv,
           ssem, rsem):
    t, r = lax.axis_index("tensor"), lax.axis_index("replay")
    c, yh, z = lax.rem(t, 2), lax.rem(t // 2, 2), t // 4
    x, yl = r // 4, lax.rem(r, 4)
    h = lax.rem(z, 2)

    def device(x_, yl_, yh_, z_, c_):
        return ((z_ * 2 + yh_) * 2 + c_, x_ * 4 + yl_)

    def xat(k):
        return lax.rem(x + k + 4, 4)

    def yat(k):
        return lax.rem(yl + k + 4, 4)

    def zat(k):
        return lax.rem(z + k + 8, 8)

    xdev = {k: device(xat(k), yl, yh, z, c) for k in (1, -1)}
    zdev = {k: device(x, yl, yh, zat(k), c) for k in (1, -1)}
    ydev = {k: device(x, yat(k), yh, z, c) for k in (1, 2, 3)}
    sib = device(x, yl, yh, z, 1 - c)
    q = 2 * h + yh
    zt = 2 * (z // 2) + yl // 2
    alone = yl == q
    yhs = (yh, 1 - yh)
    to_dev = [device(x, q, v, zt, c) for v in yhs]
    from_dev = [device(x, 2 * h + v, lax.rem(yl, 2), zt, c) for v in yhs]

    bar = pltpu.get_barrier_semaphore()
    peers = list(xdev.values()) + list(zdev.values()) + list(ydev.values()) + [sib]
    for d in peers + to_dev + from_dev:
        pl.semaphore_signal(bar, inc=1, device_id=d, device_id_type=MESH)

    sent = []

    def desc(src, dst, s, rs, dev):
        return pltpu.make_async_remote_copy(
            src_ref=src, dst_ref=dst, send_sem=ssem.at[s], recv_sem=rsem.at[rs],
            device_id=dev, device_id_type=MESH)

    def send(src, dst, dev, *key):
        s = LABEL(*key)
        cp = desc(src, dst, s, s, dev)
        cp.start()
        sent.append(cp)

    def arrive(dst, *key):
        s = LABEL(*key)
        desc(dst, dst, s, s, sib).wait_recv()

    iota0 = lax.broadcasted_iota(jnp.int32, (ROWS, ROWS), 0)
    iota1 = lax.broadcasted_iota(jnp.int32, (ROWS, ROWS), 1)
    pick = jnp.where(iota0 == idx_ref[...], 1.0, 0.0).astype(BF)
    eye = jnp.where(iota0 == iota1, 1.0, 0.0).astype(BF)
    own[0] = dot(pick, x_ref[...], 0, 0).astype(BF)
    own[1] = do_ref[...]
    dh[yl, 0:QF] = dot(dq_ref[...], eye, 0, 0).astype(BF)
    dh[yl, QF:QO] = dot(a_ref[...], pick, 0, 0).astype(BF)
    wall[x, 0:QF] = wq_ref[...]
    wall[x, QF:QO] = wo_ref[...]
    pl.semaphore_wait(bar, len(peers) + 4)

    def turn(arr):
        dst = xb.at[arr, c, zt, pl.ds(pl.multiple_of(lax.rem(yl, 2) * ROWS, ROWS), ROWS)]
        rs = LABEL("turn", arr, 0) + lax.rem(yl, 2)
        assert LABEL("turn", arr, 1) == LABEL("turn", arr, 0) + 1

        @pl.when(alone)
        def _():
            pltpu.make_async_copy(own.at[arr], dst, rsem.at[rs]).start()

        @pl.when(jnp.logical_not(alone))
        def _():
            desc(own.at[arr], dst, LABEL("turn", arr, 0), rs, to_dev[0]).start()

        desc(own.at[arr], dst, LABEL("turn", arr, 1), rs, to_dev[1]).start()

    def turn_sent(arr):
        @pl.when(jnp.logical_not(alone))
        def _():
            desc(own.at[arr], own.at[arr], LABEL("turn", arr, 0), 0, to_dev[0]).wait_send()

        desc(own.at[arr], own.at[arr], LABEL("turn", arr, 1), 0, to_dev[1]).wait_send()

    turn(0)
    for k in (1, 2, 3):
        send(dh.at[yl], dh.at[yl], ydev[k], "dh", k)
    turn(1)
    for k in (1, -1):
        send(wall.at[x], wall.at[x], xdev[k], "w", k)

    def zvalid(step, arr, way):
        return step < 4 or (arr == 0) == (way == 1)

    def zpass(step, arr):
        for way in (1, -1):
            if zvalid(step, arr, way):
                at = zat(-way * (step - 1))
                send(xb.at[arr, c, at], xb.at[arr, c, at], zdev[way], "z", step, arr, way)

    def ztake(step, arr):
        for way in (1, -1):
            if zvalid(step, arr, way):
                at = zat(-way * step)
                arrive(xb.at[arr, c, at], "z", step, arr, way)

    def zgive(step, arr):
        for way in (1, -1):
            if zvalid(step, arr, way):
                at = zat(-way * step)
                send(xb.at[arr, c, at], xb.at[arr, c, at], sib, "s", step, arr, way)

    for arr in (0, 1):
        for v in (0, 1):
            arrive(xb.at[arr, c, z, pl.ds(v * ROWS, ROWS)], "turn", arr, v)
        zpass(1, arr)
        send(xb.at[arr, c, z], xb.at[arr, c, z], sib, "s", 0, arr)

    A, B = (0, QO // 2), (QO // 2, QO // 2)
    for k, half in ((1, A), (-1, B)):
        arrive(wall.at[xat(-k)], "w", k)
        piece = wall.at[xat(-k), pl.ds(*half)]
        send(piece, piece, xdev[k], "w2", k)

    for step in (1, 2, 3):
        for arr in (0, 1):
            ztake(step, arr)
            zpass(step + 1, arr)
            zgive(step, arr)
    for arr in (0, 1):
        ztake(4, arr)
        zgive(4, arr)

    for k in (1, 2, 3):
        arrive(dh.at[yat(-k)], "dh", k)

    def other(arr):
        arrive(xb.at[arr, 1 - c, z], "s", 0, arr)
        for step in (1, 2, 3, 4):
            for way in (1, -1):
                if zvalid(step, arr, way):
                    arrive(xb.at[arr, 1 - c, zat(-way * step)], "s", step, arr, way)

    def block(arr, xp):
        return jnp.concatenate(
            [jnp.concatenate([xb[arr, 0, 2 * xp + v], xb[arr, 1, 2 * xp + v]], axis=1) for v in (0, 1)], axis=0)

    def grads(p):
        lo, n = PARTS[p]
        half = n // 2
        lhs = jnp.concatenate([dh[g, lo:lo + n] for g in range(4)], axis=1)

        def term(k):
            return dot(lhs, block(p, xat(k)), 1, 0) * (1.0 / ROWS)

        gsend[lo:lo + n] = term(2).astype(BF)
        for k, at in ((1, lo), (-1, lo + half)):
            send(gsend.at[pl.ds(at, half)], gr1.at[pl.ds(at, half)], xdev[k], "g1", p, k)
        for i, k in enumerate((1, -1, 0)):
            gkeep[i, lo:lo + n] = term(k)

    def grads2(p):
        lo, n = PARTS[p]
        half = n // 2
        for i, (k, at) in enumerate(((1, lo), (-1, lo + half))):
            arrive(gr1.at[pl.ds(at, half)], "g1", p, k)
            rest = lo + half if k == 1 else lo
            gacc[i, at:at + half] = (gkeep[i, at:at + half] + gr1[at:at + half].astype(F32)).astype(BF)
            gacc[i, rest:rest + half] = gkeep[i, rest:rest + half].astype(BF)
            send(gacc.at[i, pl.ds(lo, n)], gr2.at[i, pl.ds(lo, n)], xdev[k], "g2", p, k)

    def grads3(p):
        lo, n = PARTS[p]
        for i, k in enumerate((1, -1)):
            arrive(gr2.at[i, pl.ds(lo, n)], "g2", p, k)
        gout[r, lo:lo + n] = (gkeep[2, lo:lo + n] + gr2[0, lo:lo + n].astype(F32)
                              + gr2[1, lo:lo + n].astype(F32)).astype(BF)
        piece = gout.at[r, pl.ds(lo, n)]
        for k in (1, -1):
            send(piece, piece, xdev[k], "ax", p, 0, k)
        for k in (1, 2, 3):
            send(piece, piece, ydev[k], "ay", p, k)

    def gather_y(p, j):
        lo, n = PARTS[p]
        piece = gout.at[x * 4 + yat(-j), pl.ds(lo, n)]
        arrive(piece, "ay", p, j)
        for k in (1, -1):
            send(piece, piece, xdev[k], "ax", p, j, k)

    def gather_x(p, j):
        lo, n = PARTS[p]
        half = n // 2
        for k, at in ((1, lo), (-1, lo + half)):
            row = xat(-k) * 4 + yat(-j)
            arrive(gout.at[row, pl.ds(lo, n)], "ax", p, j, k)
            piece = gout.at[row, pl.ds(at, half)]
            send(piece, piece, xdev[k], "ar", p, j, k)

    def gather_end(p, j):
        lo, n = PARTS[p]
        half = n // 2
        for k, at in ((1, lo), (-1, lo + half)):
            arrive(gout.at[xat(2) * 4 + yat(-j), pl.ds(at, half)], "ar", p, j, k)

    other(0)
    grads(0)
    other(1)
    grads(1)

    for k, half in ((1, A), (-1, B)):
        arrive(wall.at[xat(2), pl.ds(*half)], "w2", k)
    for arr, (lo, n) in enumerate(PARTS):
        w = jnp.concatenate([wall[v, lo:lo + n] for v in range(4)], axis=1)
        for g in range(4):
            y = dot(dh[g, lo:lo + n], w, 0, 0)
            rows = slice(g % 2 * ROWS, g % 2 * ROWS + ROWS)
            for xp in range(4):
                left, right = y[:, xp * 256:xp * 256 + 128], y[:, xp * 256 + 128:xp * 256 + 256]
                part[arr, 2 * xp + g // 2, rows] = jnp.where(c == 0, left, right)
                esend[arr, 2 * xp + g // 2, rows] = jnp.where(c == 0, right, left).astype(BF)
        send(esend.at[arr], erecv.at[arr], sib, "e", arr)

    grads2(0)
    grads2(1)

    for arr, (lo, n) in enumerate(PARTS):
        w = jnp.concatenate([wall[v, lo:lo + n] for v in range(4)], axis=1)
        for v in (0, 1):
            rhs = jnp.concatenate([xb[arr, cc, 2 * xp + v] for xp in range(4) for cc in (0, 1)], axis=1)
            y = dot(w, rhs, 1, 1)
            for j in (0, 1):
                ykeep[2 * v + j, lo:lo + n] = y[:, j * ROWS:(j + 1) * ROWS]
                ysend[2 * v + j, lo:lo + n] = y[:, j * ROWS:(j + 1) * ROWS].astype(BF)
    for k in (1, 2, 3):
        send(ysend.at[yat(k)], yrecv.at[k - 1], ydev[k], "y", k)

    def zadd(step):
        for arr in (0, 1):
            if step == 1:
                arrive(erecv.at[arr], "e", arr)
                for v in range(8):
                    part[arr, v] = part[arr, v] + erecv[arr, v].astype(F32)
            for way in (1, -1):
                i = (1 - way) // 2
                if step == 1 and (arr == 0) != (way == 1):
                    continue
                at = zat(way * (5 - step))
                value = part[arr, at]
                if step > 2 or (step == 2 and (arr == 0) == (way == 1)):
                    arrive(zrecv.at[arr, i, step - 2], "r", step - 1, arr, way)
                    value = value + zrecv[arr, i, step - 2].astype(F32)
                zsend[arr, i, step - 1] = value.astype(BF)
                send(zsend.at[arr, i, step - 1], zrecv.at[arr, i, step - 1], zdev[way], "r", step, arr, way)

    def zend():
        for arr in (0, 1):
            value = part[arr, z]
            for way in (1, -1):
                i = (1 - way) // 2
                arrive(zrecv.at[arr, i, 3], "r", 4, arr, way)
                value = value + zrecv[arr, i, 3].astype(F32)
            value = value.astype(BF)
            for j in (0, 1):
                scsend[j, arr] = value[j * ROWS:(j + 1) * ROWS]

    def scatter():
        rs = LABEL("sc", 0) + yh
        assert LABEL("sc", 1) == LABEL("sc", 0) + 1
        dst = screcv.at[yh]

        @pl.when(alone)
        def _():
            pltpu.make_async_copy(scsend.at[yhs[0]], dst, rsem.at[rs]).start()

        @pl.when(jnp.logical_not(alone))
        def _():
            desc(scsend.at[yhs[0]], dst, LABEL("sc", 0), rs, from_dev[0]).start()

        desc(scsend.at[yhs[1]], dst, LABEL("sc", 1), rs, from_dev[1]).start()

    def scatter_end():
        for v in (0, 1):
            arrive(screcv.at[v], "sc", v)
        gin_ref[...] = screcv[0, 0].astype(F32) + screcv[1, 0].astype(F32)
        out_ref[...] = screcv[0, 1].astype(F32) + screcv[1, 1].astype(F32)

        @pl.when(jnp.logical_not(alone))
        def _():
            desc(scsend.at[0], scsend.at[0], LABEL("sc", 0), 0, from_dev[0]).wait_send()

        desc(scsend.at[0], scsend.at[0], LABEL("sc", 1), 0, from_dev[1]).wait_send()

    zadd(1)
    grads3(0)
    grads3(1)
    zadd(2)
    for p in (0, 1):
        gather_y(p, 1)
    for p in (0, 1):
        gather_x(p, 0)
    zadd(3)
    for p in (0, 1):
        gather_y(p, 2)
        gather_y(p, 3)
    zadd(4)
    for p in (0, 1):
        gather_x(p, 1)
    zend()
    scatter()
    for p in (0, 1):
        gather_x(p, 2)

    total = ykeep[yl]
    for k in (1, 2, 3):
        arrive(yrecv.at[k - 1], "y", k)
        total = total + yrecv[k - 1].astype(F32)
    qkv_ref[...] = total[0:QF].T
    gat_ref[...] = total[QF:QO].T

    for p in (0, 1):
        gather_x(p, 3)
    scatter_end()
    for p in (0, 1):
        for j in range(4):
            gather_end(p, j)
    for row in range(16):
        gwq_ref[:, row * 256:(row + 1) * 256] = gout[row, 0:QF]
        gwo_ref[:, row * 256:(row + 1) * 256] = gout[row, QF:QO]
    turn_sent(0)
    turn_sent(1)
    for cp in sent:
        cp.wait_send()


def shards(*args):
    vm = pl.BlockSpec(memory_space=pltpu.VMEM)
    shapes = [((ROWS, QF), F32), ((ROWS, OF), F32), ((ROWS, 128), F32), ((ROWS, 128), F32),
              ((QF, 4096), BF), ((OF, 4096), BF)]
    scratch = [
        ((2, ROWS, 128), BF),
        ((4, QO, ROWS), BF),
        ((4, QO, 256), BF),
        ((2, 2, 8, 256, 128), BF),
        ((QO, 256), BF),
        ((3, QO, 256), F32),
        ((2, QO, 256), BF),
        ((QO, 256), BF),
        ((2, QO, 256), BF),
        ((16, QO, 256), BF),
        ((4, QO, ROWS), BF),
        ((3, QO, ROWS), BF),
        ((4, QO, ROWS), F32),
        ((2, 8, 256, 128), BF),
        ((2, 8, 256, 128), BF),
        ((2, 8, 256, 128), F32),
        ((2, 2, 4, 256, 128), BF),
        ((2, 2, 4, 256, 128), BF),
        ((2, 2, ROWS, 128), BF),
        ((2, 2, ROWS, 128), BF),
    ]
    count = 160
    return tuple(pl.pallas_call(
        kernel,
        name="critic_layer",
        out_shape=[jax.ShapeDtypeStruct(s, d) for s, d in shapes],
        in_specs=[vm] * 7,
        out_specs=[vm] * 6,
        scratch_shapes=[pltpu.VMEM(s, d) for s, d in scratch]
        + [pltpu.SemaphoreType.DMA((count,)), pltpu.SemaphoreType.DMA((count,))],
        compiler_params=pltpu.CompilerParams(
            collective_id=0, has_side_effects=True, vmem_limit_bytes=40 << 20),
    )(*args))


def solution(mesh):
    in_specs = (
        P("replay", "tensor"),
        P("replay", "tensor"),
        P("replay", None),
        P("tensor", "replay"),
        P("tensor", "replay"),
        P("replay", "tensor"),
        P("replay", "tensor"),
    )
    out_specs = (
        P("replay", "tensor"),
        P("replay", "tensor"),
        P("replay", "tensor"),
        P("replay", "tensor"),
        P("tensor", None),
        P("tensor", None),
    )
    return jax.shard_map(shards, mesh=mesh, in_specs=in_specs, out_specs=out_specs, check_vma=False)
```

time: 787 us -> 96.5 us (0.12)
  the two profiles are of different devices: /device:TPU:1 before, /device:TPU:48 now
where the time goes in v1:
time: 96.5 us; the launch traced here: 96 us
  Pallas kernels  85 us (88%)
  local copies, waits for them, and re-layouts  10.3 us (11%)
    pallas_call x1, Pallas kernels, shards(): pl.pallas_call(kernel, name='critic_layer', out_shape=[jax.ShapeDtypeStru...  85 us
    unnamed x18, local copies, waits for them, and re-layouts  9.55 us

profile of v1, /device:TPU:48, one launch (start us, length us, event | category | flops | bytes accessed | tf_op | source)
XLA Modules:
  0.0 96.0 jit_solution(14886239693785483112)
XLA Ops:
  0.6 0.9 copy.13.dq_ref
  1.5 0.0 copy-start
  1.5 0.9 copy-done
  2.4 0.0 copy-start.1
  2.4 0.8 copy-done.1
  3.3 0.0 copy-start.2
  3.3 0.8 copy-done.2
  4.0 0.0 copy-start.3
  4.0 0.8 copy-done.3
  4.8 0.0 copy-start.4
  4.8 0.8 copy-done.4
  5.5 0.0 copy-start.5
  5.5 0.7 copy-done.5
  6.2 85.0 %critic_layer.1 = (f32[128,192]{1,0:T(8,128)S(1)}, f32[128,128]{1,0:T(8,128)S(1)}, f32[128,128]{1,0:T(8,128)S(1)}, f32[128,128]{1,0:T(8,128)S(1)}, bf16[192,4096...) custom-call(bf16[128,128]{1,0:T(8,128)(2,1)S(1)} %copy-done.2, bf16[128,128]{1,0:T(8,128)(2,1)S(1)} %copy-done.3, ...), custom_call_target="tpu_custom_call" | custom-call | tf_op jit(solution)/shard_map/critic_layer/pallas_call | solution.py:397
  91.3 0.7 copy.14
  92.0 0.6 copy.20
  92.6 0.6 copy.21
  93.3 0.6 copy.22
  93.9 1.1 %copy.23 = bf16[192,4096]{1,0:T(8,128)(2,1)} copy(bf16[192,4096]{1,0:T(8,128)(2,1)S(1)} %get-tuple-element.22) | data formatting | bytes 3145728
  95.0 1.0 %copy.24 = bf16[128,4096]{1,0:T(8,128)(2,1)} copy(bf16[128,4096]{1,0:T(8,128)(2,1)S(1)} %get-tuple-element.23) | data formatting | bytes 2097152
Async XLA Ops:
  1.5 0.9 copy-start
  2.4 0.8 copy-start.1
  3.3 0.8 copy-start.2
  4.0 0.8 copy-start.3
  4.8 0.8 copy-start.4
  5.5 0.7 copy-start.5

commit v2 on v1

--- a/solution.py
+++ b/solution.py
@@ -29,9 +29,9 @@
 
 def kernel(x_ref, a_ref, idx_ref, wq_ref, wo_ref, dq_ref, do_ref,
            qkv_ref, out_ref, gin_ref, gat_ref, gwq_ref, gwo_ref,
-           own, dh, wall, xb, gsend, gkeep, gacc, gr1, gr2, gout,
+           xin, ain, idx, own, dh, wall, xb, gsend, gkeep, gr, gout,
            ysend, yrecv, ykeep, esend, erecv, part, zsend, zrecv, scsend, screcv,
-           ssem, rsem):
+           ssem, rsem, lsem):
     t, r = lax.axis_index("tensor"), lax.axis_index("replay")
     c, yh, z = lax.rem(t, 2), lax.rem(t // 2, 2), t // 4
     x, yl = r // 4, lax.rem(r, 4)
@@ -49,7 +49,7 @@
     def zat(k):
         return lax.rem(z + k + 8, 8)
 
-    xdev = {k: device(xat(k), yl, yh, z, c) for k in (1, -1)}
+    xdev = {k: device(xat(k), yl, yh, z, c) for k in (1, -1, 2)}
     zdev = {k: device(x, yl, yh, zat(k), c) for k in (1, -1)}
     ydev = {k: device(x, yat(k), yh, z, c) for k in (1, 2, 3)}
     sib = device(x, yl, yh, z, 1 - c)
@@ -60,6 +60,16 @@
     to_dev = [device(x, q, v, zt, c) for v in yhs]
     from_dev = [device(x, 2 * h + v, lax.rem(yl, 2), zt, c) for v in yhs]
 
+    loads = [
+        pltpu.make_async_copy(src, dst, lsem.at[i])
+        for i, (src, dst) in enumerate((
+            (idx_ref, idx), (x_ref, xin), (do_ref, own.at[1]),
+            (wq_ref, wall.at[x, pl.ds(0, QF)]), (wo_ref, wall.at[x, pl.ds(QF, OF)]),
+            (dq_ref, dh.at[yl, pl.ds(0, QF)]), (a_ref, ain)))
+    ]
+    for cp in loads:
+        cp.start()
+
     bar = pltpu.get_barrier_semaphore()
     peers = list(xdev.values()) + list(zdev.values()) + list(ydev.values()) + [sib]
     for d in peers + to_dev + from_dev:
@@ -83,15 +93,13 @@
         desc(dst, dst, s, s, sib).wait_recv()
 
     iota0 = lax.broadcasted_iota(jnp.int32, (ROWS, ROWS), 0)
-    iota1 = lax.broadcasted_iota(jnp.int32, (ROWS, ROWS), 1)
-    pick = jnp.where(iota0 == idx_ref[...], 1.0, 0.0).astype(BF)
-    eye = jnp.where(iota0 == iota1, 1.0, 0.0).astype(BF)
-    own[0] = dot(pick, x_ref[...], 0, 0).astype(BF)
-    own[1] = do_ref[...]
-    dh[yl, 0:QF] = dot(dq_ref[...], eye, 0, 0).astype(BF)
-    dh[yl, QF:QO] = dot(a_ref[...], pick, 0, 0).astype(BF)
-    wall[x, 0:QF] = wq_ref[...]
-    wall[x, QF:QO] = wo_ref[...]
+    loads[0].wait()
+    loads[1].wait()
+    pick = jnp.where(iota0 == idx[...], 1.0, 0.0).astype(BF)
+    own[0] = dot(pick, xin[...], 0, 0).astype(BF)
+    for cp in loads[2:]:
+        cp.wait()
+    dh[yl, QF:QO] = dot(ain[...], pick, 0, 0).astype(BF)
     pl.semaphore_wait(bar, len(peers) + 4)
 
     def turn(arr):
@@ -117,63 +125,57 @@
         desc(own.at[arr], own.at[arr], LABEL("turn", arr, 1), 0, to_dev[1]).wait_send()
 
     turn(0)
+    turn(1)
+    for k in (1, -1, 2):
+        send(wall.at[x], wall.at[x], xdev[k], "w", k)
+
+    def zways(step, arr):
+        return [w for w in (1, -1) if step < 4 or (arr == 0) == (w == 1)]
+
+    def zblock(core, step, arr, way, v):
+        return xb.at[arr, core, zat(-way * step), pl.ds(v * ROWS, ROWS)]
+
+    def zpass(step, arr, way, v):
+        if way in zways(step, arr):
+            piece = zblock(c, step - 1, arr, way, v)
+            send(piece, piece, zdev[way], "z", step, arr, way, v)
+
+    def zgive(step, arr, way, v):
+        piece = zblock(c, step, arr, way, v)
+        send(piece, piece, sib, "s", step, arr, way, v)
+
+    def zfirst(arr):
+        for v in (0, 1):
+            arrive(zblock(c, 0, arr, 1, v), "turn", arr, v)
+            for way in (1, -1):
+                zpass(1, arr, way, v)
+        for v in (0, 1):
+            zgive(0, arr, 1, v)
+
+    def zstep(step, arr):
+        for v in (0, 1):
+            for way in zways(step, arr):
+                arrive(zblock(c, step, arr, way, v), "z", step, arr, way, v)
+                if step < 4:
+                    zpass(step + 1, arr, way, v)
+        for v in (0, 1):
+            for way in zways(step, arr):
+                zgive(step, arr, way, v)
+
+    zfirst(0)
     for k in (1, 2, 3):
         send(dh.at[yl], dh.at[yl], ydev[k], "dh", k)
-    turn(1)
-    for k in (1, -1):
-        send(wall.at[x], wall.at[x], xdev[k], "w", k)
-
-    def zvalid(step, arr, way):
-        return step < 4 or (arr == 0) == (way == 1)
-
-    def zpass(step, arr):
-        for way in (1, -1):
-            if zvalid(step, arr, way):
-                at = zat(-way * (step - 1))
-                send(xb.at[arr, c, at], xb.at[arr, c, at], zdev[way], "z", step, arr, way)
-
-    def ztake(step, arr):
-        for way in (1, -1):
-            if zvalid(step, arr, way):
-                at = zat(-way * step)
-                arrive(xb.at[arr, c, at], "z", step, arr, way)
-
-    def zgive(step, arr):
-        for way in (1, -1):
-            if zvalid(step, arr, way):
-                at = zat(-way * step)
-                send(xb.at[arr, c, at], xb.at[arr, c, at], sib, "s", step, arr, way)
-
+    zfirst(1)
     for arr in (0, 1):
-        for v in (0, 1):
-            arrive(xb.at[arr, c, z, pl.ds(v * ROWS, ROWS)], "turn", arr, v)
-        zpass(1, arr)
-        send(xb.at[arr, c, z], xb.at[arr, c, z], sib, "s", 0, arr)
-
-    A, B = (0, QO // 2), (QO // 2, QO // 2)
-    for k, half in ((1, A), (-1, B)):
-        arrive(wall.at[xat(-k)], "w", k)
-        piece = wall.at[xat(-k), pl.ds(*half)]
-        send(piece, piece, xdev[k], "w2", k)
-
-    for step in (1, 2, 3):
-        for arr in (0, 1):
-            ztake(step, arr)
-            zpass(step + 1, arr)
-            zgive(step, arr)
-    for arr in (0, 1):
-        ztake(4, arr)
-        zgive(4, arr)
-
-    for k in (1, 2, 3):
-        arrive(dh.at[yat(-k)], "dh", k)
+        zstep(1, arr)
 
     def other(arr):
-        arrive(xb.at[arr, 1 - c, z], "s", 0, arr)
+        for v in (0, 1):
+            arrive(zblock(1 - c, 0, arr, 1, v), "s", 0, arr, 1, v)
         for step in (1, 2, 3, 4):
-            for way in (1, -1):
-                if zvalid(step, arr, way):
-                    arrive(xb.at[arr, 1 - c, zat(-way * step)], "s", step, arr, way)
+            for v in (0, 1):
+                for way in zways(step, arr):
+                    arrive(zblock(1 - c, step, arr, way, v), "s", step, arr, way, v)
 
     def block(arr, xp):
         return jnp.concatenate(
@@ -181,34 +183,23 @@
 
     def grads(p):
         lo, n = PARTS[p]
-        half = n // 2
         lhs = jnp.concatenate([dh[g, lo:lo + n] for g in range(4)], axis=1)
 
         def term(k):
             return dot(lhs, block(p, xat(k)), 1, 0) * (1.0 / ROWS)
 
-        gsend[lo:lo + n] = term(2).astype(BF)
-        for k, at in ((1, lo), (-1, lo + half)):
-            send(gsend.at[pl.ds(at, half)], gr1.at[pl.ds(at, half)], xdev[k], "g1", p, k)
-        for i, k in enumerate((1, -1, 0)):
-            gkeep[i, lo:lo + n] = term(k)
+        for i, k in enumerate((2, 1, -1)):
+            gsend[i, lo:lo + n] = term(k).astype(BF)
+            send(gsend.at[i, pl.ds(lo, n)], gr.at[i, pl.ds(lo, n)], xdev[k], "g", p, k)
+        gkeep[lo:lo + n] = term(0)
 
     def grads2(p):
         lo, n = PARTS[p]
-        half = n // 2
-        for i, (k, at) in enumerate(((1, lo), (-1, lo + half))):
-            arrive(gr1.at[pl.ds(at, half)], "g1", p, k)
-            rest = lo + half if k == 1 else lo
-            gacc[i, at:at + half] = (gkeep[i, at:at + half] + gr1[at:at + half].astype(F32)).astype(BF)
-            gacc[i, rest:rest + half] = gkeep[i, rest:rest + half].astype(BF)
-            send(gacc.at[i, pl.ds(lo, n)], gr2.at[i, pl.ds(lo, n)], xdev[k], "g2", p, k)
-
-    def grads3(p):
-        lo, n = PARTS[p]
-        for i, k in enumerate((1, -1)):
-            arrive(gr2.at[i, pl.ds(lo, n)], "g2", p, k)
-        gout[r, lo:lo + n] = (gkeep[2, lo:lo + n] + gr2[0, lo:lo + n].astype(F32)
-                              + gr2[1, lo:lo + n].astype(F32)).astype(BF)
+        total = gkeep[lo:lo + n]
+        for i, k in enumerate((2, 1, -1)):
+            arrive(gr.at[i, pl.ds(lo, n)], "g", p, k)
+            total = total + gr[i, lo:lo + n].astype(F32)
+        gout[r, lo:lo + n] = total.astype(BF)
         piece = gout.at[r, pl.ds(lo, n)]
         for k in (1, -1):
             send(piece, piece, xdev[k], "ax", p, 0, k)
@@ -237,14 +228,8 @@
         for k, at in ((1, lo), (-1, lo + half)):
             arrive(gout.at[xat(2) * 4 + yat(-j), pl.ds(at, half)], "ar", p, j, k)
 
-    other(0)
-    grads(0)
-    other(1)
-    grads(1)
-
-    for k, half in ((1, A), (-1, B)):
-        arrive(wall.at[xat(2), pl.ds(*half)], "w2", k)
-    for arr, (lo, n) in enumerate(PARTS):
+    def eterm(arr):
+        lo, n = PARTS[arr]
         w = jnp.concatenate([wall[v, lo:lo + n] for v in range(4)], axis=1)
         for g in range(4):
             y = dot(dh[g, lo:lo + n], w, 0, 0)
@@ -255,10 +240,8 @@
                 esend[arr, 2 * xp + g // 2, rows] = jnp.where(c == 0, right, left).astype(BF)
         send(esend.at[arr], erecv.at[arr], sib, "e", arr)
 
-    grads2(0)
-    grads2(1)
-
-    for arr, (lo, n) in enumerate(PARTS):
+    def yterm(arr):
+        lo, n = PARTS[arr]
         w = jnp.concatenate([wall[v, lo:lo + n] for v in range(4)], axis=1)
         for v in (0, 1):
             rhs = jnp.concatenate([xb[arr, cc, 2 * xp + v] for xp in range(4) for cc in (0, 1)], axis=1)
@@ -266,8 +249,8 @@
             for j in (0, 1):
                 ykeep[2 * v + j, lo:lo + n] = y[:, j * ROWS:(j + 1) * ROWS]
                 ysend[2 * v + j, lo:lo + n] = y[:, j * ROWS:(j + 1) * ROWS].astype(BF)
-    for k in (1, 2, 3):
-        send(ysend.at[yat(k)], yrecv.at[k - 1], ydev[k], "y", k)
+        for k in (1, 2, 3):
+            send(ysend.at[yat(k), pl.ds(lo, n)], yrecv.at[k - 1, pl.ds(lo, n)], ydev[k], "y", arr, k)
 
     def zadd(step):
         for arr in (0, 1):
@@ -325,35 +308,53 @@
 
         desc(scsend.at[0], scsend.at[0], LABEL("sc", 1), 0, from_dev[1]).wait_send()
 
+    for arr in (0, 1):
+        zstep(2, arr)
+    for k in (1, -1, 2):
+        arrive(wall.at[xat(-k)], "w", k)
+    for k in (1, 2, 3):
+        arrive(dh.at[yat(-k)], "dh", k)
+    eterm(0)
+    for arr in (0, 1):
+        zstep(3, arr)
+    eterm(1)
+    for arr in (0, 1):
+        zstep(4, arr)
+    other(0)
+    grads(0)
+    other(1)
+    grads(1)
     zadd(1)
-    grads3(0)
-    grads3(1)
+    yterm(0)
+    yterm(1)
+    grads2(0)
+    grads2(1)
     zadd(2)
-    for p in (0, 1):
-        gather_y(p, 1)
-    for p in (0, 1):
-        gather_x(p, 0)
+    gather_y(0, 1)
+    gather_x(0, 0)
+    gather_y(1, 1)
+    gather_x(1, 0)
     zadd(3)
-    for p in (0, 1):
-        gather_y(p, 2)
-        gather_y(p, 3)
+    gather_y(0, 2)
+    gather_y(0, 3)
+    gather_x(0, 1)
+    gather_y(1, 2)
+    gather_y(1, 3)
+    gather_x(1, 1)
     zadd(4)
-    for p in (0, 1):
-        gather_x(p, 1)
+    gather_x(0, 2)
+    gather_x(0, 3)
     zend()
     scatter()
-    for p in (0, 1):
-        gather_x(p, 2)
-
+    gather_x(1, 2)
+    gather_x(1, 3)
     total = ykeep[yl]
     for k in (1, 2, 3):
-        arrive(yrecv.at[k - 1], "y", k)
+        for arr, (lo, n) in enumerate(PARTS):
+            arrive(yrecv.at[k - 1, pl.ds(lo, n)], "y", arr, k)
         total = total + yrecv[k - 1].astype(F32)
-    qkv_ref[...] = total[0:QF].T
+    qkv_ref[...] = total[0:QF]
     gat_ref[...] = total[QF:QO].T
-
-    for p in (0, 1):
-        gather_x(p, 3)
     scatter_end()
     for p in (0, 1):
         for j in range(4):
@@ -367,20 +368,30 @@
         cp.wait_send()
 
 
-def shards(*args):
-    vm = pl.BlockSpec(memory_space=pltpu.VMEM)
-    shapes = [((ROWS, QF), F32), ((ROWS, OF), F32), ((ROWS, 128), F32), ((ROWS, 128), F32),
+def spread(*refs):
+    n = len(refs) // 2
+    copies = [pltpu.make_async_copy(refs[i], refs[n + i], refs[2 * n].at[i]) for i in range(n)]
+    for cp in copies:
+        cp.start()
+    for cp in copies:
+        cp.wait()
+
+
+def shards(x_store, attn_store, replay_idx, w_qkv, w_out, d_qkv, d_out):
+    vm, hbm = pl.BlockSpec(memory_space=pltpu.VMEM), pl.BlockSpec(memory_space=pl.ANY)
+    shapes = [((QF, ROWS), F32), ((ROWS, 128), F32), ((ROWS, 128), F32), ((ROWS, 128), F32),
               ((QF, 4096), BF), ((OF, 4096), BF)]
     scratch = [
+        ((ROWS, 128), BF),
+        ((ROWS, 128), BF),
+        ((1, ROWS), jnp.int32),
         ((2, ROWS, 128), BF),
         ((4, QO, ROWS), BF),
         ((4, QO, 256), BF),
         ((2, 2, 8, 256, 128), BF),
-        ((QO, 256), BF),
-        ((3, QO, 256), F32),
-        ((2, QO, 256), BF),
-        ((QO, 256), BF),
-        ((2, QO, 256), BF),
+        ((3, QO, 256), BF),
+        ((QO, 256), F32),
+        ((3, QO, 256), BF),
         ((16, QO, 256), BF),
         ((4, QO, ROWS), BF),
         ((3, QO, ROWS), BF),
@@ -393,18 +404,29 @@
         ((2, 2, ROWS, 128), BF),
         ((2, 2, ROWS, 128), BF),
     ]
-    count = 160
-    return tuple(pl.pallas_call(
+    count = 200
+    parts = pl.pallas_call(
         kernel,
         name="critic_layer",
         out_shape=[jax.ShapeDtypeStruct(s, d) for s, d in shapes],
-        in_specs=[vm] * 7,
+        in_specs=[hbm] * 7,
         out_specs=[vm] * 6,
         scratch_shapes=[pltpu.VMEM(s, d) for s, d in scratch]
-        + [pltpu.SemaphoreType.DMA((count,)), pltpu.SemaphoreType.DMA((count,))],
+        + [pltpu.SemaphoreType.DMA((n,)) for n in (count, count, 7)],
         compiler_params=pltpu.CompilerParams(
-            collective_id=0, has_side_effects=True, vmem_limit_bytes=40 << 20),
-    )(*args))
+            collective_id=0, has_side_effects=True, vmem_limit_bytes=48 << 20),
+    )(*(pltpu.with_memory_space_constraint(v, pltpu.HBM)
+        for v in (x_store, attn_store, replay_idx, w_qkv, w_out, d_qkv.T, d_out)))
+    qkv, *rest = pl.pallas_call(
+        spread,
+        name="spread",
+        out_shape=[jax.ShapeDtypeStruct(s, d) for s, d in shapes],
+        in_specs=[hbm] * 6,
+        out_specs=[hbm] * 6,
+        scratch_shapes=[pltpu.SemaphoreType.DMA((6,))],
+        compiler_params=pltpu.CompilerParams(vmem_limit_bytes=1 << 20),
+    )(*parts)
+    return (qkv.T, *rest)
 
 
 def solution(mesh):

time: 96.5 us -> 81.8 us (0.85)
  the two profiles are of different devices: /device:TPU:48 before, /device:TPU:16 now
where the time goes in v2:
time: 81.8 us; the launch traced here: 81.7 us
  Pallas kernels  81 us (99%)
    pallas_call x1, Pallas kernels, shards(): pl.pallas_call(kernel, name='critic_layer', out_shape=[jax.ShapeDtypeStru...  79.4 us
    pallas_call x1, Pallas kernels, shards(): pl.pallas_call(spread, name='spread', out_shape=[jax.ShapeDtypeStruct(s,...  1.64 us

profile of v2, /device:TPU:16, one launch (start us, length us, event | category | flops | bytes accessed | tf_op | source)
XLA Modules:
  0.0 81.7 jit_solution(11649826002270344672)
XLA Ops:
  0.6 79.4 %critic_layer.1 = (f32[192,128]{1,0:T(8,128)S(1)}, f32[128,128]{1,0:T(8,128)S(1)}, f32[128,128]{1,0:T(8,128)S(1)}, f32[128,128]{1,0:T(8,128)S(1)}, bf16[192,4096...) custom-call(bf16[128,128]{1,0:T(8,128)(2,1)} %x_ref.1, bf16[128,128]{1,0:T(8,128)(2,1)} %a_ref.1, s32[1,128]{1,0:T(1,128)} %idx_ref.1, ...), custom_call_target="tpu_custom_call" | custom-call | tf_op jit(solution)/shard_map/critic_layer/pallas_call | solution.py:408
  80.0 1.6 %spread.1 = (f32[192,128]{1,0:T(8,128)}, f32[128,128]{1,0:T(8,128)}, f32[128,128]{1,0:T(8,128)}, f32[128,128]{1,0:T(8,128)}, bf16[192,4096]{1,0:T(8,128)(2,1)}, /*index=5*/bf16[128,4096]{1,0:T(8,128)(2,1)}) custom-call(f32[192,128]{1,0:T(8,128)S(1)} %get-tuple-element.18.refs_0_, f32[128,128]{1,0:T(8,128)S(1)} %get-tuple-element.19.refs_1_, ...), custom_call_target="tpu_custom_call" | custom-call | tf_op jit(solution)/shard_map/spread/pallas_call | solution.py:420

commit v3 on v2

--- a/solution.py
+++ b/solution.py
@@ -9,6 +9,7 @@
 MESH = pl.DeviceIdType.MESH
 ROWS, QF, OF, QO = 128, 192, 128, 320
 PARTS = ((0, QF), (QF, OF))
+PIECES = ((0, 96), (96, 96), (192, 64), (256, 64))
 
 
 def dot(a, b, ca, cb):
@@ -76,6 +77,11 @@
         pl.semaphore_signal(bar, inc=1, device_id=d, device_id_type=MESH)
 
     sent = []
+    near = jnp.where(yl == 0, 3, 1)
+    slot_y = (yl, yat(2), yat(-near), yat(near))
+    inner = jnp.logical_and(yl > 0, yl < 3)
+    end = 3 * (yl // 2)
+    ends = []
 
     def desc(src, dst, s, rs, dev):
         return pltpu.make_async_remote_copy(
@@ -102,6 +108,32 @@
     dh[yl, QF:QO] = dot(ain[...], pick, 0, 0).astype(BF)
     pl.semaphore_wait(bar, len(peers) + 4)
 
+    def line(block, *key):
+        first = LABEL(*key, 1)
+        assert (LABEL(*key, 2), LABEL(*key, 3)) == (first + 1, first + 2)
+
+        def go(k, slot):
+            s = LABEL(*key, "k", k)
+            return desc(block(yl), block(yl), s, first + slot - 1, ydev[k])
+
+        go(2, 1).start()
+        pl.when(yl != 3)(lambda: go(1, 2).start())
+        pl.when(yl != 0)(lambda: go(3, jnp.where(yl == 1, 2, 3)).start())
+        ends.append(lambda: go(2, 1).wait_send())
+        ends.append(lambda: pl.when(yl != 3)(lambda: go(1, 2).wait_send()))
+        ends.append(lambda: pl.when(yl != 0)(lambda: go(3, 3).wait_send()))
+
+    def line_take(block, slot, *key):
+        arrive(block(slot_y[slot]), *key, slot)
+        if slot == 1:
+            s = LABEL(*key, "k", 0)
+
+            def go():
+                return desc(block(yat(2)), block(yat(2)), s, LABEL(*key, 3), device(x, end, yh, z, c))
+
+            pl.when(inner)(lambda: go().start())
+            ends.append(lambda: pl.when(inner)(lambda: go().wait_send()))
+
     def turn(arr):
         dst = xb.at[arr, c, zt, pl.ds(pl.multiple_of(lax.rem(yl, 2) * ROWS, ROWS), ROWS)]
         rs = LABEL("turn", arr, 0) + lax.rem(yl, 2)
@@ -161,13 +193,6 @@
         for v in (0, 1):
             for way in zways(step, arr):
                 zgive(step, arr, way, v)
-
-    zfirst(0)
-    for k in (1, 2, 3):
-        send(dh.at[yl], dh.at[yl], ydev[k], "dh", k)
-    zfirst(1)
-    for arr in (0, 1):
-        zstep(1, arr)
 
     def other(arr):
         for v in (0, 1):
@@ -200,33 +225,37 @@
             arrive(gr.at[i, pl.ds(lo, n)], "g", p, k)
             total = total + gr[i, lo:lo + n].astype(F32)
         gout[r, lo:lo + n] = total.astype(BF)
-        piece = gout.at[r, pl.ds(lo, n)]
-        for k in (1, -1):
-            send(piece, piece, xdev[k], "ax", p, 0, k)
-        for k in (1, 2, 3):
-            send(piece, piece, ydev[k], "ay", p, k)
-
-    def gather_y(p, j):
-        lo, n = PARTS[p]
-        piece = gout.at[x * 4 + yat(-j), pl.ds(lo, n)]
-        arrive(piece, "ay", p, j)
-        for k in (1, -1):
-            send(piece, piece, xdev[k], "ax", p, j, k)
-
-    def gather_x(p, j):
-        lo, n = PARTS[p]
+        for piece in (2 * p, 2 * p + 1):
+            lo, n = PIECES[piece]
+            mine = gout.at[r, pl.ds(lo, n)]
+            for k in (1, -1):
+                send(mine, mine, xdev[k], "ax", piece, 0, k)
+            line(lambda y: gout.at[x * 4 + y, pl.ds(lo, n)], "ay", piece)
+
+    def gather_y(p, *slots):
+        lo, n = PIECES[p]
+        for slot in slots:
+            line_take(lambda y: gout.at[x * 4 + y, pl.ds(lo, n)], slot, "ay", p)
+            piece = gout.at[x * 4 + slot_y[slot], pl.ds(lo, n)]
+            for k in (1, -1):
+                send(piece, piece, xdev[k], "ax", p, slot, k)
+
+    def gather_x(p, *slots):
+        lo, n = PIECES[p]
         half = n // 2
-        for k, at in ((1, lo), (-1, lo + half)):
-            row = xat(-k) * 4 + yat(-j)
-            arrive(gout.at[row, pl.ds(lo, n)], "ax", p, j, k)
-            piece = gout.at[row, pl.ds(at, half)]
-            send(piece, piece, xdev[k], "ar", p, j, k)
-
-    def gather_end(p, j):
-        lo, n = PARTS[p]
+        for slot in slots:
+            for k, at in ((1, lo), (-1, lo + half)):
+                row = xat(-k) * 4 + slot_y[slot]
+                arrive(gout.at[row, pl.ds(lo, n)], "ax", p, slot, k)
+                piece = gout.at[row, pl.ds(at, half)]
+                send(piece, piece, xdev[k], "ar", p, slot, k)
+
+    def gather_end(p):
+        lo, n = PIECES[p]
         half = n // 2
-        for k, at in ((1, lo), (-1, lo + half)):
-            arrive(gout.at[xat(2) * 4 + yat(-j), pl.ds(at, half)], "ar", p, j, k)
+        for slot in range(4):
+            for k, at in ((1, lo), (-1, lo + half)):
+                arrive(gout.at[xat(2) * 4 + slot_y[slot], pl.ds(at, half)], "ar", p, slot, k)
 
     def eterm(arr):
         lo, n = PARTS[arr]
@@ -249,6 +278,9 @@
             for j in (0, 1):
                 ykeep[2 * v + j, lo:lo + n] = y[:, j * ROWS:(j + 1) * ROWS]
                 ysend[2 * v + j, lo:lo + n] = y[:, j * ROWS:(j + 1) * ROWS].astype(BF)
+
+    def ygo(arr):
+        lo, n = PARTS[arr]
         for k in (1, 2, 3):
             send(ysend.at[yat(k), pl.ds(lo, n)], yrecv.at[k - 1, pl.ds(lo, n)], ydev[k], "y", arr, k)
 
@@ -308,46 +340,55 @@
 
         desc(scsend.at[0], scsend.at[0], LABEL("sc", 1), 0, from_dev[1]).wait_send()
 
+    def dhblock(y):
+        return dh.at[y]
+
+    zfirst(0)
+    line(dhblock, "dh")
+    zfirst(1)
+    for arr in (0, 1):
+        zstep(1, arr)
     for arr in (0, 1):
         zstep(2, arr)
+    line_take(dhblock, 1, "dh")
+    for arr in (0, 1):
+        zstep(3, arr)
+    line_take(dhblock, 2, "dh")
+    line_take(dhblock, 3, "dh")
+    zstep(4, 0)
+    other(0)
+    grads(0)
+    zstep(4, 1)
+    other(1)
+    grads(1)
     for k in (1, -1, 2):
         arrive(wall.at[xat(-k)], "w", k)
-    for k in (1, 2, 3):
-        arrive(dh.at[yat(-k)], "dh", k)
     eterm(0)
-    for arr in (0, 1):
-        zstep(3, arr)
     eterm(1)
-    for arr in (0, 1):
-        zstep(4, arr)
-    other(0)
-    grads(0)
-    other(1)
-    grads(1)
+    yterm(0)
+    ygo(0)
+    yterm(1)
     zadd(1)
-    yterm(0)
-    yterm(1)
     grads2(0)
     grads2(1)
     zadd(2)
-    gather_y(0, 1)
     gather_x(0, 0)
-    gather_y(1, 1)
+    gather_y(0, 1, 2, 3)
     gather_x(1, 0)
+    gather_y(1, 1, 2, 3)
     zadd(3)
-    gather_y(0, 2)
-    gather_y(0, 3)
-    gather_x(0, 1)
-    gather_y(1, 2)
-    gather_y(1, 3)
-    gather_x(1, 1)
+    gather_x(0, 1, 2, 3)
+    gather_x(2, 0)
+    gather_y(2, 1, 2, 3)
+    gather_x(1, 1, 2, 3)
+    gather_x(3, 0)
+    gather_y(3, 1, 2, 3)
     zadd(4)
-    gather_x(0, 2)
-    gather_x(0, 3)
+    ygo(1)
+    gather_x(2, 1, 2, 3)
     zend()
     scatter()
-    gather_x(1, 2)
-    gather_x(1, 3)
+    gather_x(3, 1, 2, 3)
     total = ykeep[yl]
     for k in (1, 2, 3):
         for arr, (lo, n) in enumerate(PARTS):
@@ -356,9 +397,8 @@
     qkv_ref[...] = total[0:QF]
     gat_ref[...] = total[QF:QO].T
     scatter_end()
-    for p in (0, 1):
-        for j in range(4):
-            gather_end(p, j)
+    for p in range(4):
+        gather_end(p)
     for row in range(16):
         gwq_ref[:, row * 256:(row + 1) * 256] = gout[row, 0:QF]
         gwo_ref[:, row * 256:(row + 1) * 256] = gout[row, QF:QO]
@@ -366,6 +406,8 @@
     turn_sent(1)
     for cp in sent:
         cp.wait_send()
+    for wait in ends:
+        wait()
 
 
 def spread(*refs):
@@ -404,7 +446,7 @@
         ((2, 2, ROWS, 128), BF),
         ((2, 2, ROWS, 128), BF),
     ]
-    count = 200
+    count = 240
     parts = pl.pallas_call(
         kernel,
         name="critic_layer",

time: 81.8 us -> 77.3 us (0.945)
  the two profiles are of different devices: /device:TPU:16 before, /device:TPU:1 now
where the time goes in v3:
time: 77.3 us; the launch traced here: 76.2 us
  Pallas kernels  75.5 us (98%)
    pallas_call x1, Pallas kernels, shards(): pl.pallas_call(kernel, name='critic_layer', out_shape=[jax.ShapeDtypeStru...  73.9 us
    pallas_call x1, Pallas kernels, shards(): pl.pallas_call(spread, name='spread', out_shape=[jax.ShapeDtypeStruct(s,...  1.64 us

profile of v3, /device:TPU:1, one launch (start us, length us, event | category | flops | bytes accessed | tf_op | source)
XLA Modules:
  0.0 76.2 jit_solution(7838545794797875150)
XLA Ops:
  0.6 73.9 %critic_layer.1 = (f32[192,128]{1,0:T(8,128)S(1)}, f32[128,128]{1,0:T(8,128)S(1)}, f32[128,128]{1,0:T(8,128)S(1)}, f32[128,128]{1,0:T(8,128)S(1)}, bf16[192,4096...) custom-call(bf16[128,128]{1,0:T(8,128)(2,1)} %x_ref.1, bf16[128,128]{1,0:T(8,128)(2,1)} %a_ref.1, s32[1,128]{1,0:T(1,128)} %idx_ref.1, ...), custom_call_target="tpu_custom_call" | custom-call | tf_op jit(solution)/shard_map/critic_layer/pallas_call | solution.py:450
  74.5 1.6 %spread.1 = (f32[192,128]{1,0:T(8,128)}, f32[128,128]{1,0:T(8,128)}, f32[128,128]{1,0:T(8,128)}, f32[128,128]{1,0:T(8,128)}, bf16[192,4096]{1,0:T(8,128)(2,1)}, /*index=5*/bf16[128,4096]{1,0:T(8,128)(2,1)}) custom-call(f32[192,128]{1,0:T(8,128)S(1)} %get-tuple-element.18.refs_0_, f32[128,128]{1,0:T(8,128)S(1)} %get-tuple-element.19.refs_1_, ...), custom_call_target="tpu_custom_call" | custom-call | tf_op jit(solution)/shard_map/spread/pallas_call | solution.py:462

commit v4 on v3

--- a/solution.py
+++ b/solution.py
@@ -103,9 +103,6 @@
     loads[1].wait()
     pick = jnp.where(iota0 == idx[...], 1.0, 0.0).astype(BF)
     own[0] = dot(pick, xin[...], 0, 0).astype(BF)
-    for cp in loads[2:]:
-        cp.wait()
-    dh[yl, QF:QO] = dot(ain[...], pick, 0, 0).astype(BF)
     pl.semaphore_wait(bar, len(peers) + 4)
 
     def line(block, *key):
@@ -157,7 +154,10 @@
         desc(own.at[arr], own.at[arr], LABEL("turn", arr, 1), 0, to_dev[1]).wait_send()
 
     turn(0)
+    for cp in loads[2:]:
+        cp.wait()
     turn(1)
+    dh[yl, QF:QO] = dot(ain[...], pick, 0, 0).astype(BF)
     for k in (1, -1, 2):
         send(wall.at[x], wall.at[x], xdev[k], "w", k)
 
@@ -165,6 +165,8 @@
         return [w for w in (1, -1) if step < 4 or (arr == 0) == (w == 1)]
 
     def zblock(core, step, arr, way, v):
+        if v is None:
+            return xb.at[arr, core, zat(-way * step)]
         return xb.at[arr, core, zat(-way * step), pl.ds(v * ROWS, ROWS)]
 
     def zpass(step, arr, way, v):
@@ -179,28 +181,23 @@
     def zfirst(arr):
         for v in (0, 1):
             arrive(zblock(c, 0, arr, 1, v), "turn", arr, v)
-            for way in (1, -1):
-                zpass(1, arr, way, v)
-        for v in (0, 1):
-            zgive(0, arr, 1, v)
+        for way in (1, -1):
+            zpass(1, arr, way, None)
+        zgive(0, arr, 1, None)
 
     def zstep(step, arr):
-        for v in (0, 1):
+        for way in zways(step, arr):
+            arrive(zblock(c, step, arr, way, None), "z", step, arr, way, None)
+            if step < 4:
+                zpass(step + 1, arr, way, None)
+        for way in zways(step, arr):
+            zgive(step, arr, way, None)
+
+    def other(arr):
+        arrive(zblock(1 - c, 0, arr, 1, None), "s", 0, arr, 1, None)
+        for step in (1, 2, 3, 4):
             for way in zways(step, arr):
-                arrive(zblock(c, step, arr, way, v), "z", step, arr, way, v)
-                if step < 4:
-                    zpass(step + 1, arr, way, v)
-        for v in (0, 1):
-            for way in zways(step, arr):
-                zgive(step, arr, way, v)
-
-    def other(arr):
-        for v in (0, 1):
-            arrive(zblock(1 - c, 0, arr, 1, v), "s", 0, arr, 1, v)
-        for step in (1, 2, 3, 4):
-            for v in (0, 1):
-                for way in zways(step, arr):
-                    arrive(zblock(1 - c, step, arr, way, v), "s", step, arr, way, v)
+                arrive(zblock(1 - c, step, arr, way, None), "s", step, arr, way, None)
 
     def block(arr, xp):
         return jnp.concatenate(
@@ -249,6 +246,13 @@
                 arrive(gout.at[row, pl.ds(lo, n)], "ax", p, slot, k)
                 piece = gout.at[row, pl.ds(at, half)]
                 send(piece, piece, xdev[k], "ar", p, slot, k)
+
+    def put(k):
+        for y in range(4):
+            row = xat(k) * 4 + y
+            cols = pl.ds(pl.multiple_of(row * 256, 256), 256)
+            gwq_ref[:, cols] = gout[row, 0:QF]
+            gwo_ref[:, cols] = gout[row, QF:QO]
 
     def gather_end(p):
         lo, n = PIECES[p]
@@ -345,50 +349,74 @@
 
     zfirst(0)
     line(dhblock, "dh")
+
     zfirst(1)
+
     for arr in (0, 1):
         zstep(1, arr)
+
     for arr in (0, 1):
         zstep(2, arr)
+
     line_take(dhblock, 1, "dh")
     for arr in (0, 1):
         zstep(3, arr)
+
     line_take(dhblock, 2, "dh")
     line_take(dhblock, 3, "dh")
+
+    for k in (1, -1, 2):
+        arrive(wall.at[xat(-k)], "w", k)
+    eterm(0)
     zstep(4, 0)
     other(0)
+
     grads(0)
+
+    eterm(1)
+    yterm(0)
+    ygo(0)
+
     zstep(4, 1)
     other(1)
     grads(1)
-    for k in (1, -1, 2):
-        arrive(wall.at[xat(-k)], "w", k)
-    eterm(0)
-    eterm(1)
-    yterm(0)
-    ygo(0)
     yterm(1)
+    ygo(1)
+
     zadd(1)
+
     grads2(0)
+
+    zadd(2)
+
     grads2(1)
-    zadd(2)
+
     gather_x(0, 0)
     gather_y(0, 1, 2, 3)
+
+    zadd(3)
     gather_x(1, 0)
     gather_y(1, 1, 2, 3)
-    zadd(3)
+
     gather_x(0, 1, 2, 3)
+    zadd(4)
     gather_x(2, 0)
     gather_y(2, 1, 2, 3)
+
+    zend()
+    scatter()
+
     gather_x(1, 1, 2, 3)
     gather_x(3, 0)
     gather_y(3, 1, 2, 3)
-    zadd(4)
-    ygo(1)
+
     gather_x(2, 1, 2, 3)
-    zend()
-    scatter()
+
+    put(0)
     gather_x(3, 1, 2, 3)
+    put(1)
+    put(-1)
+
     total = ykeep[yl]
     for k in (1, 2, 3):
         for arr, (lo, n) in enumerate(PARTS):
@@ -396,12 +424,13 @@
         total = total + yrecv[k - 1].astype(F32)
     qkv_ref[...] = total[0:QF]
     gat_ref[...] = total[QF:QO].T
+
     scatter_end()
+
     for p in range(4):
         gather_end(p)
-    for row in range(16):
-        gwq_ref[:, row * 256:(row + 1) * 256] = gout[row, 0:QF]
-        gwo_ref[:, row * 256:(row + 1) * 256] = gout[row, QF:QO]
+
+    put(2)
     turn_sent(0)
     turn_sent(1)
     for cp in sent:

time: 77.3 us -> 76.1 us (0.984); the launches traced: 76.2 us -> 76 us
  no operation moved by 1% of the time
where the time goes in v4:
time: 76.1 us; the launch traced here: 76 us
  Pallas kernels  75.3 us (99%)
    pallas_call x1, Pallas kernels, shards(): pl.pallas_call(kernel, name='critic_layer', out_shape=[jax.ShapeDtypeStru...  73.7 us
    pallas_call x1, Pallas kernels, shards(): pl.pallas_call(spread, name='spread', out_shape=[jax.ShapeDtypeStruct(s,...  1.64 us

profile of v4, /device:TPU:1, one launch (start us, length us, event | category | flops | bytes accessed | tf_op | source)
XLA Modules:
  0.0 76.0 jit_solution(15850208279663214035)
XLA Ops:
  0.6 73.7 %critic_layer.1 = (f32[192,128]{1,0:T(8,128)S(1)}, f32[128,128]{1,0:T(8,128)S(1)}, f32[128,128]{1,0:T(8,128)S(1)}, f32[128,128]{1,0:T(8,128)S(1)}, bf16[192,4096...) custom-call(bf16[128,128]{1,0:T(8,128)(2,1)} %x_ref.1, bf16[128,128]{1,0:T(8,128)(2,1)} %a_ref.1, s32[1,128]{1,0:T(1,128)} %idx_ref.1, ...), custom_call_target="tpu_custom_call" | custom-call | tf_op jit(solution)/shard_map/critic_layer/pallas_call | solution.py:479
  74.3 1.6 %spread.1 = (f32[192,128]{1,0:T(8,128)}, f32[128,128]{1,0:T(8,128)}, f32[128,128]{1,0:T(8,128)}, f32[128,128]{1,0:T(8,128)}, bf16[192,4096]{1,0:T(8,128)(2,1)}, /*index=5*/bf16[128,4096]{1,0:T(8,128)(2,1)}) custom-call(f32[192,128]{1,0:T(8,128)S(1)} %get-tuple-element.18.refs_0_, f32[128,128]{1,0:T(8,128)S(1)} %get-tuple-element.19.refs_1_, ...), custom_call_target="tpu_custom_call" | custom-call | tf_op jit(solution)/shard_map/spread/pallas_call | solution.py:491

commit v5 on v4

--- a/solution.py
+++ b/solution.py
@@ -225,9 +225,9 @@
         for piece in (2 * p, 2 * p + 1):
             lo, n = PIECES[piece]
             mine = gout.at[r, pl.ds(lo, n)]
+            line(lambda y: gout.at[x * 4 + y, pl.ds(lo, n)], "ay", piece)
             for k in (1, -1):
                 send(mine, mine, xdev[k], "ax", piece, 0, k)
-            line(lambda y: gout.at[x * 4 + y, pl.ds(lo, n)], "ay", piece)
 
     def gather_y(p, *slots):
         lo, n = PIECES[p]

time: 76.1 us -> 76.2 us (level)
  no operation moved by 1% of the time
where the time goes in v5:
time: 76.2 us; the launch traced here: 76 us
  Pallas kernels  75.4 us (99%)
    pallas_call x1, Pallas kernels, shards(): pl.pallas_call(kernel, name='critic_layer', out_shape=[jax.ShapeDtypeStru...  73.7 us
    pallas_call x1, Pallas kernels, shards(): pl.pallas_call(spread, name='spread', out_shape=[jax.ShapeDtypeStruct(s,...  1.64 us

profile of v5, /device:TPU:1, one launch (start us, length us, event | category | flops | bytes accessed | tf_op | source)
XLA Modules:
  0.0 76.0 jit_solution(6227964561865321217)
XLA Ops:
  0.6 73.7 %critic_layer.1 = (f32[192,128]{1,0:T(8,128)S(1)}, f32[128,128]{1,0:T(8,128)S(1)}, f32[128,128]{1,0:T(8,128)S(1)}, f32[128,128]{1,0:T(8,128)S(1)}, bf16[192,4096...) custom-call(bf16[128,128]{1,0:T(8,128)(2,1)} %x_ref.1, bf16[128,128]{1,0:T(8,128)(2,1)} %a_ref.1, s32[1,128]{1,0:T(1,128)} %idx_ref.1, ...), custom_call_target="tpu_custom_call" | custom-call | tf_op jit(solution)/shard_map/critic_layer/pallas_call | solution.py:479
  74.4 1.6 %spread.1 = (f32[192,128]{1,0:T(8,128)}, f32[128,128]{1,0:T(8,128)}, f32[128,128]{1,0:T(8,128)}, f32[128,128]{1,0:T(8,128)}, bf16[192,4096]{1,0:T(8,128)(2,1)}, /*index=5*/bf16[128,4096]{1,0:T(8,128)(2,1)}) custom-call(f32[192,128]{1,0:T(8,128)S(1)} %get-tuple-element.18.refs_0_, f32[128,128]{1,0:T(8,128)S(1)} %get-tuple-element.19.refs_1_, ...), custom_call_target="tpu_custom_call" | custom-call | tf_op jit(solution)/shard_map/spread/pallas_call | solution.py:491
